TPU v7x, 32 devices: a whole 2x2x4 slice. The times are simulated.
32 devices in a mesh: groups: 2 (over x), dp: 8 (over z, y), fsdp: 2 (over core).
Axes of the slice: x: 2, y: 2, z: 4, core: 2. Of those that a mesh axis runs over, the one named last changes fastest.
Arguments:
- hidden: bfloat16 [8192, 8192], P(('groups', 'dp', 'fsdp')), parts along dimension 0, may hold values from -600 to 600
- norm_gain: bfloat16 [8192], P('fsdp'), may hold values from 0.099609375 to 1.8984375
- w_query: bfloat16 [8192, 512], P('fsdp'), may hold values from -0.06629126 to 0.06629126
- w_key: bfloat16 [8192, 128], P('fsdp'), may hold values from -0.0625 to 0.0625
- w_value: bfloat16 [8192, 128], P('fsdp'), may hold values from -0.0625 to 0.0625
- b_query: bfloat16 [512], replicated, may hold values from -3 to 3
- b_key: bfloat16 [128], replicated, may hold values from -40 to 40
- b_value: bfloat16 [128], replicated, may hold values from -3 to 3
- row_host: int32 [8192], P(('groups', 'dp', 'fsdp')), parts along dimension 0, may hold values from 0 to 15, as said below
- row_slot: int32 [8192], P(('groups', 'dp', 'fsdp')), parts along dimension 0, may hold values from 0 to 7
Outputs:
- context: bfloat16 [8192, 512], P(('groups', 'dp', 'fsdp')), parts along dimension 0
There are 2 independent parts, one for each index of `groups`. A program takes and returns all parts, laid end to end along the dimension named above; an argument that names none is the same for every part. Nothing has to cross between parts.
Inputs may be any that keep to these rules, and one draw needn't show every extreme that they name: `row_host`: index of the hosting device along dp and fsdp together. Of one device's rows at most 32 go to one host; in every draw some host receives exactly 32 rows from every device.
All inputs are finite; a program needn't handle non-finite values.
Results may differ from a plain program's by a relative error of at most 0.012.
The roundings to bfloat16 on the way count: a program that leaves them out, or rounds other values in their place, can miss the bound.
Values may be sent and summed in bfloat16 or wider, within the bound.
No kernel may reach another device: no remote copies, remote signals or barrier semaphores. Data moves between devices by JAX's collectives and lax.ppermute only.
A program may use at most 128 MiB of HBM per device.

v0:
```python
import jax
import jax.numpy as jnp
from jax import lax
from jax.sharding import PartitionSpec as P

HD = 128
HQ = 4


rope_base = 1000000.0
epsilon = 1e-06


def rotary(tensor, position):
    half_dim = tensor.shape[-1] // 2
    frequency = jnp.power(
        rope_base, -jnp.arange(half_dim, dtype=jnp.float32) * 2.0 / tensor.shape[-1]
    )
    rotation = position.astype(jnp.float32)[:, None] * frequency[None, :]
    cosine = jnp.cos(rotation)[:, None, :]
    sine_part = jnp.sin(rotation)[:, None, :]
    front_half = tensor[..., :half_dim]
    back_half = tensor[..., half_dim:]
    return jnp.concatenate(
        [front_half * cosine - back_half * sine_part, back_half * cosine + front_half * sine_part],
        axis=-1,
    )


def finish(query_sum, key_sum, value_sum, b_query, b_key, b_value):
    return jnp.concatenate(
        [
            (query_sum + b_query.astype(jnp.float32)).astype(jnp.bfloat16),
            (key_sum + b_key.astype(jnp.float32)).astype(jnp.bfloat16),
            (value_sum + b_value.astype(jnp.float32)).astype(jnp.bfloat16),
        ],
        axis=1,
    )


def project(source_rows, norm_gain, w_query, w_key, w_value, b_query, b_key, b_value):
    widened = source_rows.astype(jnp.float32)
    inverse = lax.rsqrt(jnp.mean(widened * widened, axis=1, keepdims=True) + epsilon)
    query_part = lax.all_gather(w_query, "fsdp", axis=0, tiled=True)
    key_part = lax.all_gather(w_key, "fsdp", axis=0, tiled=True)
    value_part = lax.all_gather(w_value, "fsdp", axis=0, tiled=True)
    gain_part = lax.all_gather(norm_gain, "fsdp", axis=0, tiled=True)
    normed_part = (
        source_rows.astype(jnp.float32) * inverse * gain_part.astype(jnp.float32)
    ).astype(jnp.bfloat16)
    query_sum = jnp.dot(normed_part, query_part, preferred_element_type=jnp.float32)
    key_sum = jnp.dot(normed_part, key_part, preferred_element_type=jnp.float32)
    value_sum = jnp.dot(normed_part, value_part, preferred_element_type=jnp.float32)
    return finish(query_sum, key_sum, value_sum, b_query, b_key, b_value)


def attend(projected, slot_ids):
    row_count = projected.shape[0]
    query_width = HQ * HD
    queries = projected[:, :query_width].reshape(row_count, HQ, HD)
    keys_raw = projected[:, query_width : query_width + HD]
    values_raw = projected[:, query_width + HD :]
    index_row = jnp.arange(row_count)
    same_slot = slot_ids[:, None] == slot_ids[None, :]
    position = jnp.sum(same_slot & (index_row[None, :] < index_row[:, None]), axis=1)
    allowed = same_slot & (index_row[None, :] <= index_row[:, None])
    query_rot = rotary(queries.astype(jnp.float32), position).astype(jnp.bfloat16)
    key_rot = rotary(keys_raw.astype(jnp.float32)[:, None, :], position)[:, 0, :].astype(
        jnp.bfloat16
    )
    scores = jnp.einsum(
        "qhd,kd->hqk", query_rot, key_rot, preferred_element_type=jnp.float32
    ) * HD ** (-0.5)
    scores = jnp.where(allowed[None, :, :], scores, -jnp.inf)
    largest = jnp.max(scores, axis=-1, keepdims=True)
    exponent = jnp.exp(scores - largest)
    attention = (exponent / jnp.sum(exponent, axis=-1, keepdims=True)).astype(jnp.bfloat16)
    context = jnp.einsum("hqk,kd->qhd", attention, values_raw, preferred_element_type=jnp.float32)
    return context.astype(jnp.bfloat16).reshape(row_count, query_width)


def per_device(
    hidden, norm_gain, w_query, w_key, w_value, b_query, b_key, b_value, row_host, row_slot
):
    host_count = lax.axis_size(("dp", "fsdp"))
    source_count = hidden.shape[0]
    capacity = 2 * source_count // host_count
    index_row = jnp.arange(source_count)
    same_host = row_host[:, None] == row_host[None, :]
    row_rank = jnp.sum(same_host & (index_row[None, :] < index_row[:, None]), axis=1)
    slot_index = row_host * capacity + row_rank
    payload = project(hidden, norm_gain, w_query, w_key, w_value, b_query, b_key, b_value)
    payload_width = payload.shape[1]
    outgoing = (
        jnp.zeros((host_count * capacity, payload_width), jnp.bfloat16).at[slot_index].set(payload)
    )
    slot_out = jnp.full((host_count * capacity,), -1, jnp.int32).at[slot_index].set(row_slot)
    arrived, slot_ids = (
        lax.all_to_all(
            outgoing.reshape(host_count, capacity, payload_width),
            ("dp", "fsdp"),
            split_axis=0,
            concat_axis=0,
            tiled=True,
        ),
        lax.all_to_all(
            slot_out.reshape(host_count, capacity),
            ("dp", "fsdp"),
            split_axis=0,
            concat_axis=0,
            tiled=True,
        ),
    )
    arrived = arrived.reshape(host_count * capacity, payload_width)
    slot_ids = slot_ids.reshape(host_count * capacity)
    context = attend(arrived, slot_ids)
    returned = lax.all_to_all(
        context.reshape(host_count, capacity, context.shape[1]),
        ("dp", "fsdp"),
        split_axis=0,
        concat_axis=0,
        tiled=True,
    )
    return returned.reshape(host_count * capacity, context.shape[1])[slot_index]


def solution(mesh):
    return jax.shard_map(
        per_device,
        mesh=mesh,
        in_specs=(
            P(("groups", "dp", "fsdp"), None),
            P("fsdp"),
            P("fsdp", None),
            P("fsdp", None),
            P("fsdp", None),
            P(),
            P(),
            P(),
            P(("groups", "dp", "fsdp")),
            P(("groups", "dp", "fsdp")),
        ),
        out_specs=P(("groups", "dp", "fsdp"), None),
        check_vma=False,
    )
```

profile of v0, /device:TPU:0, one launch (start us, length us, event | category | flops | bytes accessed | tf_op | source)
XLA Modules:
  0.0 128.8 jit_solution(1679212380418908628)
XLA Ops:
  6.6 0.7 all-gather.6.cloned.1.call-update
  7.3 0.7 all-gather.8.cloned.1.call-update
  8.1 0.7 all-gather.4.cloned.1.call-update
  9.0 1.6 %scatter_custom_fusion.1 = s32[512]{0:T(512)S(1)} fusion(s32[256]{0:T(256)S(1)} %compare_select_fusion, s32[256]{0:T(256)} %param.19, s32[]{:T(128)} %constant.8.clone.1), kind=kCustom, calls=%fused_computation.66 | custom fusion | bytes 2560 | tf_op jit(solution)/shard_map/scatter | solution.py:97
  10.5 0.7 all_to_all.13
  11.2 7.4 %all-to-all-start.1 = ((s32[16,1,32]{2,1,0:T(1,128)}), s32[16,1,32]{2,1,0:T(1,128)S(1)}, u32[]{:S(2)}, u32[]{:S(2)}) async-start(s32[16,1,32]{2,1,0:T(1,128)} %all_to_all.13), calls=%async_computation.1 | async-start | bytes 16384 | tf_op jit(solution)/shard_map/all_to_all | solution.py:106
  18.6 1.9 %all_gather.12 = bf16[8192]{0:T(1024)(128)(2,1)S(1)} all-gather(bf16[4096]{0:T(1024)(128)(2,1)S(1)} %copy-done.2), channel_id=1, replica_groups=mesh['groups'=2,'dp'=8,'fsdp'=2] {'fsdp'}, dimensions={0}, use_global_device_ids=true | all-gather | bytes 24576 | tf_op jit(solution)/shard_map/all_gather | solution.py:47
  20.6 3.1 %fusion.1 = f32[256]{0:T(256)S(1)} fusion(bf16[256,8192]{1,0:T(8,128)(2,1)} %param.10), kind=kLoop, calls=%fused_computation.6 | loop fusion | flops 6291200 | bytes 4195328 | tf_op jit(solution)/shard_map/reduce_sum | solution.py:43
  23.7 4.3 %fusion.12 = bf16[256,128]{1,0:T(8,128)(2,1)S(1)} fusion(bf16[8192,128]{1,0:T(8,128)(2,1)} %all-gather.6.cloned.1.call-done, f32[128]{0:T(128)S(1)} %convert_element_type.69, bf16[256,8192]{1,0:T(8,128)(2,1)} %param.10, f32[8192]{0:T(1024)S(1)} %convert_element_type.65, f32[256]{0:T(256)S(1)} %add_rsqrt_fusion), kind=kOutput, calls=%fused_computation.25 | convolution fusion | flops 545325056 | bytes 6391296 | tf_op jit(solution)/shard_map/dot_general | solution.py:52
  28.0 7.6 %all-gather.8.cloned.1.call-done = bf16[8192,128]{1,0:T(8,128)(2,1)} async-done(((bf16[4096,128]{1,0:T(8,128)(2,1)}), bf16[8192,128]{1,0:T(8,128)(2,1)}) %all-gather.8.cloned.1.call-update) | async-done | bytes 2097168 | tf_op jit(solution)/shard_map/all_gather | solution.py:46
  35.6 4.3 %fusion.13 = bf16[256,128]{1,0:T(8,128)(2,1)S(1)} fusion(bf16[8192,128]{1,0:T(8,128)(2,1)} %all-gather.8.cloned.1.call-done, f32[128]{0:T(128)S(1)} %convert_element_type.71, bf16[256,8192]{1,0:T(8,128)(2,1)} %param.10, f32[8192]{0:T(1024)S(1)} %convert_element_type.65, f32[256]{0:T(256)S(1)} %add_rsqrt_fusion), kind=kOutput, calls=%fused_computation.26 | convolution fusion | flops 545325056 | bytes 6391296 | tf_op jit(solution)/shard_map/dot_general | solution.py:53
  39.9 18.3 %all-gather.4.cloned.1.call-done = bf16[8192,512]{1,0:T(8,128)(2,1)} async-done(((bf16[4096,512]{1,0:T(8,128)(2,1)}), bf16[8192,512]{1,0:T(8,128)(2,1)}) %all-gather.4.cloned.1.call-update) | async-done | bytes 8388624 | tf_op jit(solution)/shard_map/all_gather | solution.py:44
  58.2 7.0 %fusion.11 = bf16[256,512]{1,0:T(8,128)(2,1)S(1)} fusion(bf16[8192,512]{1,0:T(8,128)(2,1)} %all-gather.4.cloned.1.call-done, f32[512]{0:T(512)S(1)} %convert_element_type.67, bf16[256,8192]{1,0:T(8,128)(2,1)} %param.10, f32[8192]{0:T(1024)S(1)} %convert_element_type.65, f32[256]{0:T(256)S(1)} %add_rsqrt_fusion), kind=kOutput, calls=%fused_computation.22 | convolution fusion | flops 2156134400 | bytes 12880896 | tf_op jit(solution)/shard_map/dot_general | solution.py:51
  65.2 2.6 %scatter_custom_fusion = bf16[512,768]{1,0:T(8,128)(2,1)} fusion(s32[256]{0:T(256)S(1)} %compare_select_fusion, bf16[256,128]{1,0:T(8,128)(2,1)S(1)} %fusion.13, bf16[]{:T(256)} %constant.31, bf16[256,128]{1,0:T(8,128)(2,1)S(1)} %fusion.12, bf16[256,512]{1,0:T(8,128)(2,1)S(1)} %fusion.11, bf16[]{:T(256)} %constant.12.clone.1), kind=kCustom, calls=%fused_computation.37 | custom fusion | flops 1179648 | bytes 1179652 | tf_op jit(solution)/shard_map/scatter | solution.py:95
  67.8 5.9 %all-to-all-start = ((bf16[16,32,768]{2,1,0:T(8,128)(2,1)}), bf16[16,32,768]{2,1,0:T(8,128)(2,1)S(1)}, u32[]{:S(2)}, u32[]{:S(2)}) async-start(bf16[16,32,768]{2,1,0:T(8,128)(2,1)} %bitcast), calls=%async_computation | async-start | bytes 1572864 | tf_op jit(solution)/shard_map/all_to_all | solution.py:99
  73.7 0.5 broadcast.146
  74.3 0.7 reduce.3
  75.2 0.9 compare_and_fusion.1
  76.1 1.8 %multiply_cosine_fusion = (f32[512,64]{1,0:T(8,128)}, f32[512,64]{1,0:T(8,128)}) fusion(f32[64]{0:T(128)S(1)} %multiply_power_fusion, f32[512]{0:T(512)S(1)} %convert_element_type.74), kind=kLoop, calls=%fused_computation.45 | loop fusion | flops 32768 | bytes 264448 | tf_op jit(solution)/shard_map/cos | solution.py:20
  77.9 14.5 %all-to-all-done = bf16[16,32,768]{2,1,0:T(8,128)(2,1)S(1)} async-done(((bf16[16,32,768]{2,1,0:T(8,128)(2,1)}), bf16[16,32,768]{2,1,0:T(8,128)(2,1)S(1)}, u32[]{:S(2)}, u32[]{:S(2)}) %all-to-all-start) | async-done | bytes 786464 | tf_op jit(solution)/shard_map/all_to_all | solution.py:99
  92.6 0.3 copy.51
  93.0 0.3 copy.64
  93.3 0.3 copy.65
  93.8 0.6 fusion.31
  94.4 1.3 %subtract_convert_fusion = (bf16[512,4,64]{2,0,1:T(8,128)(2,1)S(1)}, bf16[512,4,64]{2,0,1:T(8,128)(2,1)S(1)}) fusion(f32[512,4,64]{2,0,1:T(8,128)S(1)} %copy.65, f32[512,4,64]{2,0,1:T(8,128)S(1)} %copy.64, f32[512,64]{1,0:T(8,128)} %get-tuple-element.12, f32[512,64]{1,0:T(8,128)} %get-tuple-element.11), kind=kLoop, calls=%fused_computation.28 | loop fusion | flops 1048576 | bytes 1835008 | tf_op jit(solution)/shard_map/convert.2
  95.7 0.8 fusion.14
  96.6 2.1 %fusion.45 = (f32[4,512]{1,0:T(4,128)S(1)}, f32[4,512,512]{1,2,0:T(8,128)S(1)}) fusion(f32[512,512,4]{1,0,2:T(8,128)S(1)} %fusion.14, pred[512,512]{0,1:T(8,128)(4,1)S(1)} %copy-done), kind=kOutput, calls=%fused_computation.74 | output fusion | flops 6291967 | bytes 8658944 | tf_op jit(solution)/shard_map/sub | solution.py:76
  98.7 0.5 fusion.10
  99.5 1.0 reshape_reshape.3
  100.5 5.5 %all-to-all-start.2 = ((bf16[16,32,512]{2,1,0:T(8,128)(2,1)}), bf16[16,32,512]{2,1,0:T(8,128)(2,1)S(1)}, u32[]{:S(2)}, u32[]{:S(2)}) async-start(bf16[16,32,512]{2,1,0:T(8,128)(2,1)} %reshape_reshape.3), calls=%async_computation.2 | async-start | bytes 1048576 | tf_op jit(solution)/shard_map/all_to_all | solution.py:117
  106.0 14.5 %all-to-all-done.2 = bf16[16,32,512]{2,1,0:T(8,128)(2,1)S(1)} async-done(((bf16[16,32,512]{2,1,0:T(8,128)(2,1)}), bf16[16,32,512]{2,1,0:T(8,128)(2,1)S(1)}, u32[]{:S(2)}, u32[]{:S(2)}) %all-to-all-start.2) | async-done | bytes 524320 | tf_op jit(solution)/shard_map/all_to_all | solution.py:117
  120.4 1.9 %gather_fusion = bf16[256,512]{1,0:T(8,128)(2,1)} fusion(bf16[512,512]{1,0:T(8,128)(2,1)S(1)} %bitcast.32, s32[1024]{0:T(1024)S(1)} %pad_clamp_fusion), kind=kCustom, calls=%fused_computation | custom fusion | bytes 525312 | tf_op jit(solution)/shard_map/gather | solution.py:124
  (35 shorter events, 1.3 us)
Async XLA Ops:
  6.5 2.2 %copy-start.1 = (s32[256]{0:T(256)S(1)}, s32[256]{0:T(256)}, u32[]{:S(2)}) copy-start(s32[256]{0:T(256)} %param.18) | copy-start | bytes 3076
  6.5 12.1 %copy-start.2 = (bf16[4096]{0:T(1024)(128)(2,1)S(1)}, bf16[4096]{0:T(1024)(128)(2,1)}, u32[]{:S(2)}) copy-start(bf16[4096]{0:T(1024)(128)(2,1)} %param.11) | copy-start | bytes 24580
  6.5 14.0 %copy-start.3 = (bf16[512]{0:T(512)(128)(2,1)S(1)}, bf16[512]{0:T(512)(128)(2,1)}, u32[]{:S(2)}) copy-start(bf16[512]{0:T(512)(128)(2,1)} %param.15) | copy-start | bytes 3076
  6.5 14.0 %copy-start.4 = (bf16[128]{0:T(256)(128)(2,1)S(1)}, bf16[128]{0:T(256)(128)(2,1)}, u32[]{:S(2)}) copy-start(bf16[128]{0:T(256)(128)(2,1)} %param.16) | copy-start | bytes 772
  6.5 14.0 %copy-start.5 = (bf16[128]{0:T(256)(128)(2,1)S(1)}, bf16[128]{0:T(256)(128)(2,1)}, u32[]{:S(2)}) copy-start(bf16[128]{0:T(256)(128)(2,1)} %param.17) | copy-start | bytes 772
  6.5 17.2 %all-gather.6.cloned.1.call-start = ((), (), s32[]{:S(2)}) async-start(), calls=%async_computation.4 | async-start | bytes 3145728 | tf_op jit(solution)/shard_map/all_gather | solution.py:45
  7.3 28.3 %all-gather.8.cloned.1.call-start = ((), (), s32[]{:S(2)}) async-start(), calls=%async_computation.5 | async-start | bytes 3145728 | tf_op jit(solution)/shard_map/all_gather | solution.py:46
  8.0 50.1 %all-gather.4.cloned.1.call-start = ((), (), s32[]{:S(2)}) async-start(), calls=%async_computation.3 | async-start | bytes 12582912 | tf_op jit(solution)/shard_map/all_gather | solution.py:44
  11.2 56.6 %all-to-all-start.1 = ((s32[16,1,32]{2,1,0:T(1,128)}), s32[16,1,32]{2,1,0:T(1,128)S(1)}, u32[]{:S(2)}, u32[]{:S(2)}) async-start(s32[16,1,32]{2,1,0:T(1,128)} %all_to_all.13), calls=%async_computation.1 | async-start | bytes 16384 | tf_op jit(solution)/shard_map/all_to_all | solution.py:106
  67.8 24.6 %all-to-all-start = ((bf16[16,32,768]{2,1,0:T(8,128)(2,1)}), bf16[16,32,768]{2,1,0:T(8,128)(2,1)S(1)}, u32[]{:S(2)}, u32[]{:S(2)}) async-start(bf16[16,32,768]{2,1,0:T(8,128)(2,1)} %bitcast), calls=%async_computation | async-start | bytes 1572864 | tf_op jit(solution)/shard_map/all_to_all | solution.py:99
  94.4 2.2 %copy-start = (pred[512,512]{0,1:T(8,128)(4,1)S(1)}, pred[512,512]{0,1:T(8,128)(4,1)}, u32[]{:S(2)}) copy-start(pred[512,512]{0,1:T(8,128)(4,1)} %compare_and_fusion.1) | copy-start | bytes 786436
  100.5 20.0 %all-to-all-start.2 = ((bf16[16,32,512]{2,1,0:T(8,128)(2,1)}), bf16[16,32,512]{2,1,0:T(8,128)(2,1)S(1)}, u32[]{:S(2)}, u32[]{:S(2)}) async-start(bf16[16,32,512]{2,1,0:T(8,128)(2,1)} %reshape_reshape.3), calls=%async_computation.2 | async-start | bytes 1048576 | tf_op jit(solution)/shard_map/all_to_all | solution.py:117
Sparse Core Ops, SparseCore 0:
  8.9 13.2 all-gather.5
  23.8 11.7 all-gather.7
  37.1 21.0 all-gather.3
where the time goes:
time: 129 us
  waiting for transfers between devices  56.9 us (44%)
  starting transfers between devices  18.9 us (15%)
  matrix products  16.9 us (13%)
  other arithmetic  13.7 us (11%)
  between operations  13.4 us (10%)
  local copies, waits for them, and re-layouts  7.21 us (6%)
  blocking collectives  1.9 us (1%)
    all_gather x1, waiting for transfers between devices, project(): query_part = lax.all_gather(w_query, 'fsdp', axis=0, tiled=True)  18.3 us
    all_to_all x1, waiting for transfers between devices, per_device(): lax.all_to_all(outgoing.reshape(host_count, capacity, payload_width), ('d...  14.5 us
    all_to_all x1, waiting for transfers between devices, per_device(): lax.all_to_all(context.reshape(host_count, capacity, context.shape[1]), (...  14.5 us
    all_gather x1, waiting for transfers between devices, project(): value_part = lax.all_gather(w_value, 'fsdp', axis=0, tiled=True)  7.55 us
    all_to_all x1, starting transfers between devices, per_device(): lax.all_to_all(slot_out.reshape(host_count, capacity), ('dp', 'fsdp'), sp...  7.39 us
    dot_general x1, matrix products, project(): jnp.dot(normed_part, query_part, preferred_element_type=jnp.float32)  7.03 us
    all_to_all x1, starting transfers between devices, per_device(): lax.all_to_all(outgoing.reshape(host_count, capacity, payload_width), ('d...  5.9 us
    all_to_all x1, starting transfers between devices, per_device(): lax.all_to_all(context.reshape(host_count, capacity, context.shape[1]), (...  5.48 us
  transfers between devices with their start and end apart: 6, of which 4 were waited for; matrix products, arithmetic and copies ran while one was open for 21% of the time, Pallas kernels for 0%

commit v1 on v0

v1 whole, which is shorter than its diff:
```python
import functools
import jax
import jax.numpy as jnp
from jax import lax
from jax.experimental import pallas as pl
from jax.experimental.pallas import tpu as pltpu
from jax.sharding import PartitionSpec as P

HD = 128
HQ = 4
QW = HQ * HD
SLOTS_PER_HOST = 8
BLOCK = 32
rope_base = 1000000.0
epsilon = 1e-06
f32 = jnp.float32
bf16 = jnp.bfloat16
MIB = 1024 * 1024


def params(mib=40):
    return pltpu.CompilerParams(vmem_limit_bytes=mib * MIB)


def norm_kernel(core_ref, hidden_ref, gain_ref, wk_ref, wv_ref, own_ref, other_ref, pk_ref, pv_ref):
    step = pl.program_id(0)
    rows, width = hidden_ref.shape
    half = width // 2
    here = pl.multiple_of(step * rows, rows)
    core = core_ref[0]
    wide = hidden_ref[...].astype(f32)
    inverse = lax.rsqrt(jnp.sum(wide * wide, axis=1, keepdims=True) * (1.0 / width) + epsilon)

    def normed(part, gain_row):
        start = pl.multiple_of(part * half, half)
        block = hidden_ref[:, pl.ds(start, half)].astype(f32)
        return (block * inverse * gain_ref[gain_row : gain_row + 1, :].astype(f32)).astype(bf16)

    own_ref[pl.ds(here, rows), :] = normed(core, 0)
    other_ref[pl.ds(here, rows), :] = normed(1 - core, 1)

    @pl.when(step == pl.num_programs(0) - 1)
    def _():
        own = own_ref[...]
        pk_ref[...] = jnp.dot(own, wk_ref[...], preferred_element_type=f32)
        pv_ref[...] = jnp.dot(own, wv_ref[...], preferred_element_type=f32)


def norm_and_own_half(core, hidden, gains, w_key, w_value):
    rows, width = hidden.shape
    half = width // 2
    block = 32
    whole = lambda shape: pl.BlockSpec(shape, lambda i, c: (0, 0))
    return pl.pallas_call(
        norm_kernel,
        grid_spec=pltpu.PrefetchScalarGridSpec(
            num_scalar_prefetch=1,
            grid=(rows // block,),
            in_specs=[
                pl.BlockSpec((block, width), lambda i, c: (i, 0)),
                whole((2, half)),
                whole((half, HD)),
                whole((half, HD)),
            ],
            out_specs=[
                whole((rows, half)),
                whole((rows, half)),
                whole((rows, HD)),
                whole((rows, HD)),
            ],
        ),
        out_shape=[
            jax.ShapeDtypeStruct((rows, half), bf16),
            jax.ShapeDtypeStruct((rows, half), bf16),
            jax.ShapeDtypeStruct((rows, HD), f32),
            jax.ShapeDtypeStruct((rows, HD), f32),
        ],
        compiler_params=params(),
        name="norm_own_half",
    )(core, hidden, gains, w_key, w_value)


def rotate(block, cosine, sine):
    turned = jnp.concatenate([block[:, HD // 2 :], block[:, : HD // 2]], axis=1)
    return block * cosine + turned * sine


def key_value_kernel(other_ref, wk_ref, wv_ref, pk_ref, pv_ref, bk_ref, bv_ref, cos_ref, sin_ref, out_ref):
    other = other_ref[...]
    keys = pk_ref[...] + jnp.dot(other, wk_ref[...], preferred_element_type=f32)
    keys = (keys + bk_ref[...].astype(f32)).astype(bf16).astype(f32)
    out_ref[:, :HD] = rotate(keys, cos_ref[...], sin_ref[...]).astype(bf16)
    values = pv_ref[...] + jnp.dot(other, wv_ref[...], preferred_element_type=f32)
    out_ref[:, HD:] = (values + bv_ref[...].astype(f32)).astype(bf16)


def keys_and_values(other, w_key, w_value, part_key, part_value, b_key, b_value, cosine, sine):
    rows = other.shape[0]
    return pl.pallas_call(
        key_value_kernel,
        out_shape=jax.ShapeDtypeStruct((rows, 2 * HD), bf16),
        compiler_params=params(),
        name="keys_values",
    )(other, w_key, w_value, part_key, part_value, b_key[None], b_value[None], cosine, sine)


def query_kernel(own_ref, other_ref, w_own_ref, w_other_ref, b_ref, cos_ref, sin_ref, out_ref):
    total = jnp.dot(own_ref[...], w_own_ref[...], preferred_element_type=f32)
    total += jnp.dot(other_ref[...], w_other_ref[...], preferred_element_type=f32)
    total = (total + b_ref[...].astype(f32)).astype(bf16).astype(f32)
    cosine = cos_ref[...]
    sine = sin_ref[...]
    for head in range(HQ):
        at = slice(head * HD, (head + 1) * HD)
        out_ref[:, at] = rotate(total[:, at], cosine, sine).astype(bf16)


def queries_of(own, other, w_own, w_other, b_query, cosine, sine):
    rows = own.shape[0]
    return pl.pallas_call(
        query_kernel,
        out_shape=jax.ShapeDtypeStruct((rows, QW), bf16),
        compiler_params=params(),
        name="queries",
    )(own, other, w_own, w_other, b_query[None], cosine, sine)


def one_hot(slot_row, slots):
    rows = slot_row.shape[1]
    at = lax.broadcasted_iota(jnp.int32, (slots, rows), 0)
    return jnp.where(at == slot_row, 1.0, 0.0).astype(bf16)


def attention_kernel(counts, q_ref, slot_ref, key_seq_ref, query_seq_ref, *rest):
    piece_refs = rest[: len(counts)]
    out_ref, keys, values, contexts = rest[len(counts) :]
    blocks = keys.shape[0]
    slots = blocks * BLOCK

    def spread(piece, index):
        hot = one_hot(slot_ref[pl.ds(index, 1), :], slots)
        rows = jnp.dot(hot, piece, preferred_element_type=f32).astype(bf16)
        rows = rows.reshape(blocks, BLOCK, 2 * HD)
        at = pl.ds(pl.multiple_of(index * BLOCK, BLOCK), BLOCK)
        keys[:, at, :] = rows[:, :, :HD]
        values[:, at, :] = rows[:, :, HD:]

    first = 0
    for ref, count in zip(piece_refs, counts):
        if count == 1:
            spread(ref[...], first)
        else:
            lax.fori_loop(0, count, lambda i, c: (spread(ref[i], first + i), c)[1], 0)
        first += count
    total = first * BLOCK

    own_hot = one_hot(slot_ref[first : first + 1, :], slots)
    q_slots = jnp.dot(own_hot, q_ref[...], preferred_element_type=f32).astype(bf16)
    own_at = key_seq_ref[blocks : blocks + 1, :]
    q_index = lax.broadcasted_iota(jnp.int32, (HQ * BLOCK, total), 0) % BLOCK
    ordered = own_at <= q_index
    for block in range(blocks):
        rows = slice(block * BLOCK, (block + 1) * BLOCK)
        q_block = q_slots[rows, :]
        q_heads = jnp.concatenate([q_block[:, h * HD : (h + 1) * HD] for h in range(HQ)], axis=0)
        scores = lax.dot_general(
            q_heads, keys[block], (((1,), (1,)), ((), ())), preferred_element_type=f32
        ) * HD ** (-0.5)
        q_seq = query_seq_ref[rows, :]
        q_seq = jnp.concatenate([q_seq] * HQ, axis=0)
        allowed = (key_seq_ref[block : block + 1, :] == q_seq) & ordered
        scores = jnp.where(allowed, scores, -1e30)
        exponent = jnp.exp(scores - jnp.max(scores, axis=1, keepdims=True))
        weights = (exponent / jnp.sum(exponent, axis=1, keepdims=True)).astype(bf16)
        context = jnp.dot(weights, values[block], preferred_element_type=f32).astype(bf16)
        for h in range(HQ):
            contexts[rows, h * HD : (h + 1) * HD] = context[h * BLOCK : (h + 1) * BLOCK, :]
    out_ref[...] = lax.dot_general(
        own_hot, contexts[...], (((0,), (0,)), ((), ())), preferred_element_type=f32
    ).astype(bf16)


def attend(queries, slots_of_rows, key_seq, query_seq, pieces):
    rows = queries.shape[0]
    counts = tuple(1 if p.ndim == 2 else p.shape[0] for p in pieces)
    blocks = key_seq.shape[0] - 1
    total = key_seq.shape[1]
    return pl.pallas_call(
        functools.partial(attention_kernel, counts),
        out_shape=jax.ShapeDtypeStruct((rows, QW), bf16),
        scratch_shapes=[
            pltpu.VMEM((blocks, total, HD), bf16),
            pltpu.VMEM((blocks, total, HD), bf16),
            pltpu.VMEM((blocks * BLOCK, QW), bf16),
        ],
        compiler_params=params(56),
        name="attention",
    )(queries, slots_of_rows, key_seq, query_seq, *pieces)


def swap_cores(array):
    return lax.ppermute(array, "fsdp", [(0, 1), (1, 0)])


def far(array, shift, near):
    count = lax.axis_size("dp")
    return lax.ppermute(array, "dp", [(i, (i + shift * near) % count) for i in range(count)])


def swap_near(array):
    count = lax.axis_size("dp")
    return lax.ppermute(array, "dp", [(i, i ^ 1) for i in range(count)])


def stepped():
    return lax.axis_size("dp") == 8


def gather_pieces(array):
    line = [array] + [far(array, shift, 2) for shift in range(1, lax.axis_size("dp") // 2)]
    plane = line + [swap_near(a) for a in line]
    return plane + [swap_cores(a) for a in plane]


def gather_small(array):
    line = jnp.stack([array] + [far(array, shift, 2) for shift in range(1, lax.axis_size("dp") // 2)])
    plane = jnp.concatenate([line, swap_near(line)])
    return jnp.concatenate([plane, swap_cores(plane)])


def piece_sources():
    count = lax.axis_size("dp")
    row, core = lax.axis_index("dp"), lax.axis_index("fsdp")
    far_count = count // 2
    line = (((row // 2) - jnp.arange(far_count)) % far_count) * 2 + row % 2
    plane = jnp.concatenate([line, line ^ 1])
    return jnp.concatenate([plane * 2 + core, plane * 2 + 1 - core])


def per_device(
    hidden, norm_gain, w_query, w_key, w_value, b_query, b_key, b_value, row_host, row_slot
):
    host_count = lax.axis_size(("dp", "fsdp"))
    rows = hidden.shape[0]
    capacity = 2 * rows // host_count
    slots = host_count * capacity
    blocks = slots // BLOCK
    seq_count = host_count * SLOTS_PER_HOST
    core = lax.axis_index("fsdp")
    me = lax.axis_index(("dp", "fsdp"))

    index_row = jnp.arange(rows)
    lower = index_row[None, :] < index_row[:, None]
    same_host = row_host[:, None] == row_host[None, :]
    seq = row_host * SLOTS_PER_HOST + row_slot
    same_seq = seq[:, None] == seq[None, :]
    row_rank = jnp.sum(same_host & lower, axis=1, dtype=jnp.int32)
    seq_rank = jnp.sum(same_seq & lower, axis=1, dtype=jnp.int32)
    slot_index = row_host * capacity + row_rank
    slot_hot = slot_index[None, :] == jnp.arange(slots)[:, None]
    seq_of_slot = jnp.max(jnp.where(slot_hot, seq[None, :], -1), axis=1)
    seq_hot = seq[:, None] == jnp.arange(seq_count)[None, :]
    seq_size = jnp.sum(seq_hot, axis=0, dtype=jnp.int32)

    small = jnp.concatenate([slot_index, seq_of_slot, seq_size])
    if stepped():
        small_all = gather_small(small)
        sources = piece_sources()
    else:
        small_all = lax.all_gather(small, ("dp", "fsdp"))
        sources = jnp.arange(host_count)
    piece_slots = small_all[:, :rows]
    earlier = sources < me
    own = sources == me
    base = jnp.sum(jnp.where(earlier[:, None], small_all[:, rows + slots :], 0), axis=0)
    position = seq_rank + jnp.sum(jnp.where(seq_hot, base[None, :], 0), axis=1)
    key_seq = jnp.where((sources <= me)[:, None], small_all[:, rows : rows + slots], -1)
    key_seq = key_seq.reshape(host_count, blocks, BLOCK).transpose(1, 0, 2).reshape(blocks, -1)
    own_at = jnp.where(own[:, None], jnp.arange(BLOCK)[None, :], -1).reshape(1, -1)
    key_seq = jnp.concatenate([key_seq, own_at])
    query_seq = jnp.where(seq_of_slot < 0, -2, seq_of_slot)[:, None]
    slots_of_rows = jnp.concatenate([piece_slots, slot_index[None]])

    frequency = jnp.power(rope_base, -jnp.arange(HD // 2, dtype=f32) * 2.0 / HD)
    rotation = position.astype(f32)[:, None] * frequency[None, :]
    cosine, sine = jnp.cos(rotation), jnp.sin(rotation)
    cosine = jnp.concatenate([cosine, cosine], axis=1)
    sine = jnp.concatenate([-sine, sine], axis=1)

    gain_other = swap_cores(norm_gain)
    w_value_other = swap_cores(w_value)
    w_key_other = swap_cores(w_key)
    w_query_other = swap_cores(w_query)
    gains = jnp.stack([norm_gain, gain_other])
    own_half, other_half, part_key, part_value = norm_and_own_half(
        core.reshape(1), hidden, gains, w_key, w_value
    )
    pairs = keys_and_values(
        other_half, w_key_other, w_value_other, part_key, part_value, b_key, b_value, cosine, sine
    )
    if stepped():
        pieces = gather_pieces(pairs)
    else:
        pieces = [lax.all_gather(pairs, ("dp", "fsdp"))]
    queries = queries_of(own_half, other_half, w_query, w_query_other, b_query, cosine, sine)
    return attend(queries, slots_of_rows, key_seq, query_seq, pieces)


def solution(mesh):
    return jax.shard_map(
        per_device,
        mesh=mesh,
        in_specs=(
            P(("groups", "dp", "fsdp"), None),
            P("fsdp"),
            P("fsdp", None),
            P("fsdp", None),
            P("fsdp", None),
            P(),
            P(),
            P(),
            P(("groups", "dp", "fsdp")),
            P(("groups", "dp", "fsdp")),
        ),
        out_specs=P(("groups", "dp", "fsdp"), None),
        check_vma=False,
    )
```

time: 129 us -> 82.4 us (0.64)
  waiting for transfers between devices: 56.9 us -> 11.7 us
  Pallas kernels: 0 us -> 21 us
  matrix products: 16.9 us -> 0 us
  between operations: 13.4 us -> 0.36 us
  local copies, waits for them, and re-layouts: 7.21 us -> 17.1 us
  other arithmetic: 13.7 us -> 11.7 us
  blocking collectives: 1.9 us -> 0 us
    all_to_all x3 -> x0, waiting for transfers between devices: 29 us -> none  [the longest x1 14.5 us: per_device(): lax.all_to_all(outgoing.reshape(host_count, capacity, payload_width), ('d...]
    all_gather x3 -> x0, waiting for transfers between devices: 25.9 us -> none  [the longest x1 18.3 us: project(): query_part = lax.all_gather(w_query, 'fsdp', axis=0, tiled=True)]
    pallas_call x0 -> x4, Pallas kernels: none -> 21 us  [the longest x1 9.73 us: attend(): pl.pallas_call(functools.partial(attention_kernel, counts), out_shape=jax...]
    ppermute x0 -> x24, starting transfers between devices: none -> 19.7 us  [the longest x6 10.7 us: far(): lax.ppermute(array, 'dp', [(i, (i + shift * near) % count) for i in range...]
    all_to_all x3 -> x0, starting transfers between devices: 18.8 us -> none  [the longest x1 7.39 us: per_device(): lax.all_to_all(slot_out.reshape(host_count, capacity), ('dp', 'fsdp'), sp...]
    dot_general x5 -> x0, matrix products: 16.9 us -> none  [the longest x1 7.03 us: project(): jnp.dot(normed_part, query_part, preferred_element_type=jnp.float32)]
    ppermute x0 -> x24, waiting for transfers between devices: none -> 11.7 us  [the longest x6 6.32 us: far(): lax.ppermute(array, 'dp', [(i, (i + shift * near) % count) for i in range...]
    unnamed x15 -> x50, local copies, waits for them, and re-layouts: 0.8 us -> 12.5 us
  transfers between devices with their start and end apart: 6 -> 24, of which waited for: 4 -> 6; matrix products, arithmetic and copies ran while one was open for 21% -> 20% of each run, Pallas kernels for 0% -> 14%
where the time goes in v1:
time: 82.4 us; the launch traced here: 81.6 us
  Pallas kernels  21 us (25%)
  starting transfers between devices  19.7 us (24%)
  local copies, waits for them, and re-layouts  17.1 us (21%)
  other arithmetic  11.7 us (14%)
  waiting for transfers between devices  11.7 us (14%)
    unnamed x50, local copies, waits for them, and re-layouts  12.5 us
    ppermute x6, starting transfers between devices, far(): lax.ppermute(array, 'dp', [(i, (i + shift * near) % count) for i in range...  10.7 us
    pallas_call x1, Pallas kernels, attend(): pl.pallas_call(functools.partial(attention_kernel, counts), out_shape=jax...  9.73 us
    ppermute x5, starting transfers between devices, swap_near(): return lax.ppermute(array, 'dp', [(i, i ^ 1) for i in range(count)])  6.71 us
    ppermute x6, waiting for transfers between devices, far(): lax.ppermute(array, 'dp', [(i, (i + shift * near) % count) for i in range...  6.32 us
    ppermute x5, waiting for transfers between devices, swap_near(): return lax.ppermute(array, 'dp', [(i, i ^ 1) for i in range(count)])  5.37 us
    pallas_call x1, Pallas kernels, queries_of(): pl.pallas_call(query_kernel, out_shape=jax.ShapeDtypeStruct((rows, QW), b...  4.65 us
    pallas_call x1, Pallas kernels, norm_and_own_half(): pl.pallas_call(norm_kernel, grid_spec=pltpu.PrefetchScalarGridSpec(num_sc...  4.16 us
  transfers between devices with their start and end apart: 24, of which 6 were waited for; matrix products, arithmetic and copies ran while one was open for 20% of the time, Pallas kernels for 14%

profile of v1, /device:TPU:0, one launch (start us, length us, event | category | flops | bytes accessed | tf_op | source)
XLA Modules:
  0.0 81.6 jit_solution(4995799229100738812)
XLA Ops:
  0.5 0.9 %convert_reduce_fusion = s32[256]{0:T(256)S(1)} fusion(s32[256]{0:T(256)} %param.18), kind=kLoop, calls=%fused_computation.3 | loop fusion | flops 327424 | bytes 2048 | tf_op jit(solution)/shard_map/reduce_sum | solution.py:257
  2.4 2.6 %collective-permute-start.2 = (s32[896]{0:T(1024)S(1)}, s32[896]{0:T(1024)S(1)}, u32[]{:S(2)}, u32[]{:S(2)}) collective-permute-start(s32[896]{0:T(1024)S(1)} %pad_add_fusion.3), channel_id=1, source_target_pairs={{0,4},{2,6},{4,8},{6,10},{8,12},{10,14},{12,0},{14,2},{1,5},{3,7},... | collective-permute-start | bytes 10760 | tf_op jit(solution)/shard_map/ppermute | solution.py:207
  5.0 2.6 %collective-permute-start.3 = (s32[896]{0:T(1024)S(1)}, s32[896]{0:T(1024)S(1)}, u32[]{:S(2)}, u32[]{:S(2)}) collective-permute-start(s32[896]{0:T(1024)S(1)} %pad_add_fusion.3), channel_id=1, source_target_pairs={{0,8},{2,10},{4,12},{6,14},{8,0},{10,2},{12,4},{14,6},{1,9},{3,11}... | collective-permute-start | bytes 10760 | tf_op jit(solution)/shard_map/ppermute | solution.py:207
  7.6 1.3 %collective-permute-start.4 = (s32[896]{0:T(1024)S(1)}, s32[896]{0:T(1024)S(1)}, u32[]{:S(2)}, u32[]{:S(2)}) collective-permute-start(s32[896]{0:T(1024)S(1)} %pad_add_fusion.3), channel_id=1, source_target_pairs={{0,12},{2,14},{4,0},{6,2},{8,4},{10,6},{12,8},{14,10},{1,13},{3,15... | collective-permute-start | bytes 10760 | tf_op jit(solution)/shard_map/ppermute | solution.py:207
  9.1 0.8 convert_reduce_fusion.1
  11.2 1.6 %collective-permute-start.5 = (s32[4,896]{1,0:T(4,128)S(1)}, s32[4,896]{1,0:T(4,128)S(1)}, u32[]{:S(2)}, u32[]{:S(2)}) collective-permute-start(s32[4,896]{1,0:T(4,128)S(1)} %pad_add_fusion.2), channel_id=1, source_target_pairs={{0,2},{2,0},{4,6},{6,4},{8,10},{10,8},{12,14},{14,12},{1,3},{3,1},... | collective-permute-start | bytes 43016 | tf_op jit(solution)/shard_map/ppermute | solution.py:212
  15.7 2.2 %copy-done = bf16[256,8192]{1,0:T(8,128)(2,1)S(1)} copy-done((bf16[256,8192]{1,0:T(8,128)(2,1)S(1)}, bf16[256,8192]{1,0:T(8,128)(2,1)}, u32[]{:S(2)}) %copy-start) | copy-done | bytes 4194328
  17.9 1.2 %copy-done.4 = bf16[4096,128]{1,0:T(8,128)(2,1)S(1)} copy-done((bf16[4096,128]{1,0:T(8,128)(2,1)S(1)}, bf16[4096,128]{1,0:T(8,128)(2,1)}, u32[]{:S(2)}) %copy-start.4) | copy-done | bytes 1048600
  19.1 1.2 %copy-done.5 = bf16[4096,128]{1,0:T(8,128)(2,1)S(1)} copy-done((bf16[4096,128]{1,0:T(8,128)(2,1)S(1)}, bf16[4096,128]{1,0:T(8,128)(2,1)}, u32[]{:S(2)}) %copy-start.5) | copy-done | bytes 1048600
  20.4 4.2 %norm_own_half.1 = (bf16[256,4096]{1,0:T(8,128)(2,1)S(1)}, bf16[256,4096]{1,0:T(8,128)(2,1)S(1)}, f32[256,128]{1,0:T(8,128)S(1)}, f32[256,128]{1,0:T(8,128)S(1)}) custom-call(s32[1]{0:T(128)} %bitcast.core_ref, bf16[256,8192]{1,0:T(8,128)(2,1)S(1)} %copy-done, bf16[2,4096]{1,0:T(2,128)(2,1)S(1)} %pad_maximum_fusion.2.gain_ref, ...), custom_call_target="tpu_custom_call" | custom-call | tf_op jit(solution)/shard_map/norm_own_half/pallas_call | solution.py:54
  24.5 1.4 %copy-done.2 = bf16[256,4096]{1,0:T(8,128)(2,1)} copy-done((bf16[256,4096]{1,0:T(8,128)(2,1)}, bf16[256,4096]{1,0:T(8,128)(2,1)S(1)}, u32[]{:S(2)}) %copy-start.2) | copy-done | bytes 2097176
  26.9 1.1 %fusion.2 = (f32[256,64]{1,0:T(8,128)S(1)}, f32[256,64]{1,0:T(8,128)S(1)}, f32[256,64]{1,0:T(8,128)S(1)}) fusion(f32[64]{0:T(128)} %multiply_power_fusion, f32[256]{0:T(256)S(1)} %add_convert_fusion), kind=kLoop, calls=%fused_computation.17 | loop fusion | flops 32768 | bytes 197888 | tf_op jit(solution)/shard_map/neg | solution.py:288
  28.2 0.9 %copy-done.9 = f32[256,128]{1,0:T(8,128)S(1)} copy-done((f32[256,128]{1,0:T(8,128)S(1)}, f32[256,128]{1,0:T(8,128)}, u32[]{:S(2)}) %copy-start.9) | copy-done | bytes 131096
  29.1 0.9 %copy-done.11 = f32[256,128]{1,0:T(8,128)S(1)} copy-done((f32[256,128]{1,0:T(8,128)S(1)}, f32[256,128]{1,0:T(8,128)}, u32[]{:S(2)}) %copy-start.11) | copy-done | bytes 131096
  30.0 2.5 %keys_values.1.rest_0_ = bf16[256,256]{1,0:T(8,128)(2,1)S(1)} custom-call(bf16[256,4096]{1,0:T(8,128)(2,1)S(1)} %get-tuple-element.10.other_ref, bf16[4096,128]{1,0:T(8,128)(2,1)S(1)} %collective-permute-done.7.wk_ref, bf16[4096,128]{1,0:T(8,128)(2,1)} %collective-permute-done.8.wv_ref, f32[256,128]{1,0:T(8,128)S(1)} %copy-done.9, ...), custom_call_target="tpu_custom_call" | custom-call | tf_op jit(solution)/shard_map/keys_values/pallas_call | solution.py:99
  33.2 3.0 %collective-permute-start.10 = (bf16[256,256]{1,0:T(8,128)(2,1)S(1)}, bf16[256,256]{1,0:T(8,128)(2,1)S(1)}, u32[]{:S(2)}, u32[]{:S(2)}) collective-permute-start(bf16[256,256]{1,0:T(8,128)(2,1)S(1)} %keys_values.1.rest_0_), channel_id=1, source_target_pairs={{0,8},{2,10},{4,12},{6,14},{8,0},{10,2},{12,4},{14,6},{1,9},{3,11}... | collective-permute-start | bytes 393224 | tf_op jit(solution)/shard_map/ppermute | solution.py:207
  38.2 1.5 %collective-permute-start.12 = (bf16[256,256]{1,0:T(8,128)(2,1)S(1)}, bf16[256,256]{1,0:T(8,128)(2,1)S(1)}, u32[]{:S(2)}, u32[]{:S(2)}) collective-permute-start(bf16[256,256]{1,0:T(8,128)(2,1)S(1)} %keys_values.1.rest_0_), channel_id=1, source_target_pairs={{0,2},{2,0},{4,6},{6,4},{8,10},{10,8},{12,14},{14,12},{1,3},{3,1},... | collective-permute-start | bytes 393224 | tf_op jit(solution)/shard_map/ppermute | solution.py:212
  39.7 1.0 %collective-permute-done.9.rest_1_ = bf16[256,256]{1,0:T(8,128)(2,1)S(1)} collective-permute-done((bf16[256,256]{1,0:T(8,128)(2,1)S(1)}, bf16[256,256]{1,0:T(8,128)(2,1)S(1)}, u32[]{:S(2)}, u32[]{:S(2)}) %collective-permute-start.9) | collective-permute-done | bytes 131104 | tf_op jit(solution)/shard_map/ppermute | solution.py:207
  40.8 5.3 %collective-permute-done.10.rest_2_ = bf16[256,256]{1,0:T(8,128)(2,1)S(1)} collective-permute-done((bf16[256,256]{1,0:T(8,128)(2,1)S(1)}, bf16[256,256]{1,0:T(8,128)(2,1)S(1)}, u32[]{:S(2)}, u32[]{:S(2)}) %collective-permute-start.10) | collective-permute-done | bytes 131104 | tf_op jit(solution)/shard_map/ppermute | solution.py:207
  46.0 1.5 %collective-permute-start.13 = (bf16[256,256]{1,0:T(8,128)(2,1)S(1)}, bf16[256,256]{1,0:T(8,128)(2,1)S(1)}, u32[]{:S(2)}, u32[]{:S(2)}) collective-permute-start(bf16[256,256]{1,0:T(8,128)(2,1)S(1)} %collective-permute-done.9.rest_1_), channel_id=1, source_target_pairs={{0,2},{2,0},{4,6},{6,4},{8,10},{10,8},{12,14},{14,12},{1,3},{3,1},... | collective-permute-start | bytes 393224 | tf_op jit(solution)/shard_map/ppermute | solution.py:212
  49.8 1.4 %collective-permute-done.13.rest_5_ = bf16[256,256]{1,0:T(8,128)(2,1)S(1)} collective-permute-done((bf16[256,256]{1,0:T(8,128)(2,1)S(1)}, bf16[256,256]{1,0:T(8,128)(2,1)S(1)}, u32[]{:S(2)}, u32[]{:S(2)}) %collective-permute-start.13) | collective-permute-done | bytes 131104 | tf_op jit(solution)/shard_map/ppermute | solution.py:212
  51.1 1.5 %collective-permute-start.15 = (bf16[256,256]{1,0:T(8,128)(2,1)S(1)}, bf16[256,256]{1,0:T(8,128)(2,1)}, u32[]{:S(2)}, u32[]{:S(2)}) collective-permute-start(bf16[256,256]{1,0:T(8,128)(2,1)S(1)} %collective-permute-done.11.rest_3_), channel_id=1, source_target_pairs={{0,2},{2,0},{4,6},{6,4},{8,10},{10,8},{12,14},{14,12},{1,3},{3,1},... | collective-permute-start | bytes 393224 | tf_op jit(solution)/shard_map/ppermute | solution.py:212
  52.7 1.4 %slice_select_fusion = s32[16,512]{1,0:T(8,128)} fusion(s32[16,896]{1,0:T(8,128)} %copy-done.14, pred[16]{0:T(512)(128)(4,1)} %get-tuple-element.18), kind=kLoop, calls=%fused_computation.18 | loop fusion | flops 8192 | bytes 65552 | tf_op jit(solution)/shard_map/jit(_where)/select_n | solution.py:277
  54.1 1.4 %collective-permute-done.14.rest_6_ = bf16[256,256]{1,0:T(8,128)(2,1)} collective-permute-done((bf16[256,256]{1,0:T(8,128)(2,1)S(1)}, bf16[256,256]{1,0:T(8,128)(2,1)}, u32[]{:S(2)}, u32[]{:S(2)}) %collective-permute-start.14) | collective-permute-done | bytes 131104 | tf_op jit(solution)/shard_map/ppermute | solution.py:212
  55.5 2.3 %collective-permute-done.15.rest_7_ = bf16[256,256]{1,0:T(8,128)(2,1)} collective-permute-done((bf16[256,256]{1,0:T(8,128)(2,1)S(1)}, bf16[256,256]{1,0:T(8,128)(2,1)}, u32[]{:S(2)}, u32[]{:S(2)}) %collective-permute-start.15) | collective-permute-done | bytes 131104 | tf_op jit(solution)/shard_map/ppermute | solution.py:212
  59.0 1.3 %pad_add_fusion.1.slot_ref = s32[17,256]{1,0:T(8,128)} fusion(s32[1,256]{1,0:T(1,128)} %bitcast.12, s32[16,256]{1,0:T(8,128)S(1)} %slice.13), kind=kLoop, calls=%fused_computation.19 | loop fusion | flops 4352 | bytes 34816 | tf_op jit(solution)/shard_map/concatenate | solution.py:282
  60.3 0.8 %reshape.123 = s32[16,16,32]{2,1,0:T(8,128)S(1)} reshape(s32[16,512]{1,0:T(8,128)} %slice_select_fusion) | data formatting | bytes 65536 | tf_op jit(solution)/shard_map/reshape | solution.py:278
  61.3 1.3 %pad_add_fusion.key_seq_ref = s32[17,512]{1,0:T(8,128)} fusion(s32[1,512]{1,0:T(1,128)} %select_n.66, s32[16,512]{1,0:T(8,128)S(1)} %reshape.124), kind=kLoop, calls=%fused_computation.16 | loop fusion | flops 8704 | bytes 69632 | tf_op jit(solution)/shard_map/concatenate | solution.py:280
  62.6 2.2 %copy-done.1 = bf16[4096,512]{1,0:T(8,128)(2,1)S(1)} copy-done((bf16[4096,512]{1,0:T(8,128)(2,1)S(1)}, bf16[4096,512]{1,0:T(8,128)(2,1)}, u32[]{:S(2)}) %copy-start.1) | copy-done | bytes 4194328
  64.8 1.6 %copy-done.3 = bf16[256,4096]{1,0:T(8,128)(2,1)S(1)} copy-done((bf16[256,4096]{1,0:T(8,128)(2,1)S(1)}, bf16[256,4096]{1,0:T(8,128)(2,1)}, u32[]{:S(2)}) %copy-start.3) | copy-done | bytes 2097176
  66.4 4.7 %queries.1.q_ref = bf16[256,512]{1,0:T(8,128)(2,1)S(1)} custom-call(bf16[256,4096]{1,0:T(8,128)(2,1)S(1)} %copy-done.3, bf16[256,4096]{1,0:T(8,128)(2,1)S(1)} %get-tuple-element.10.other_ref, bf16[4096,512]{1,0:T(8,128)(2,1)S(1)} %copy-done.1, bf16[4096,512]{1,0:T(8,128)(2,1)} %collective-permute-done.1.w_other_ref, ...), custom_call_target="tpu_custom_call" | custom-call | tf_op jit(solution)/shard_map/queries/pallas_call | solution.py:120
  71.9 9.7 %attention.1 = bf16[256,512]{1,0:T(8,128)(2,1)} custom-call(bf16[256,512]{1,0:T(8,128)(2,1)} %copy-done.6, s32[17,256]{1,0:T(8,128)} %pad_add_fusion.1.slot_ref, s32[17,512]{1,0:T(8,128)} %pad_add_fusion.key_seq_ref, s32[512,1]{1,0:T(8,128)} %compare_select_fusion.query_seq_ref, bf16[256,256]{1,0:T(8,128)(2,1)} %copy-done.7, bf16[256,256]{1,0:T(8,128)(2,1)} %copy-done.15, ...), custom_call_target="tpu_custom_call" | custom-call | tf_op jit(solution)/shard_map/attention/pallas_call | solution.py:188
  (107 shorter events, 13.8 us)
Async XLA Ops:
  0.0 28.2 %copy-start.12 = (bf16[128]{0:T(256)(128)(2,1)S(1)}, bf16[128]{0:T(256)(128)(2,1)}, u32[]{:S(2)}) copy-start(bf16[128]{0:T(256)(128)(2,1)} %param.16) | copy-start | bytes 772
  0.0 28.2 %copy-start.13 = (bf16[128]{0:T(256)(128)(2,1)S(1)}, bf16[128]{0:T(256)(128)(2,1)}, u32[]{:S(2)}) copy-start(bf16[128]{0:T(256)(128)(2,1)} %param.17) | copy-start | bytes 772
  0.0 58.5 %collective-permute-start.1 = (bf16[4096,512]{1,0:T(8,128)(2,1)}, bf16[4096,512]{1,0:T(8,128)(2,1)}, u32[]{:S(2)}, u32[]{:S(2)}) collective-permute-start(bf16[4096,512]{1,0:T(8,128)(2,1)} %w_own_ref.1), channel_id=1, source_target_pairs={{0,1},{1,0},{2,3},{3,2},{4,5},{5,4},{6,7},{7,6},{8,9},{9,8},{10,11... | collective-permute-start | bytes 12582920 | tf_op jit(solution)/shard_map/ppermute | solution.py:202
  2.1 24.7 %copy-start.23 = (s32[256]{0:T(256)}, s32[256]{0:T(256)S(1)}, u32[]{:S(2)}) copy-start(s32[256]{0:T(256)S(1)} %get-tuple-element.23) | copy-start | bytes 3076
  2.4 8.1 %collective-permute-start.2 = (s32[896]{0:T(1024)S(1)}, s32[896]{0:T(1024)S(1)}, u32[]{:S(2)}, u32[]{:S(2)}) collective-permute-start(s32[896]{0:T(1024)S(1)} %pad_add_fusion.3), channel_id=1, source_target_pairs={{0,4},{2,6},{4,8},{6,10},{8,12},{10,14},{12,0},{14,2},{1,5},{3,7},... | collective-permute-start | bytes 10760 | tf_op jit(solution)/shard_map/ppermute | solution.py:207
  5.0 6.1 %collective-permute-start.3 = (s32[896]{0:T(1024)S(1)}, s32[896]{0:T(1024)S(1)}, u32[]{:S(2)}, u32[]{:S(2)}) collective-permute-start(s32[896]{0:T(1024)S(1)} %pad_add_fusion.3), channel_id=1, source_target_pairs={{0,8},{2,10},{4,12},{6,14},{8,0},{10,2},{12,4},{14,6},{1,9},{3,11}... | collective-permute-start | bytes 10760 | tf_op jit(solution)/shard_map/ppermute | solution.py:207
  7.6 3.6 %collective-permute-start.4 = (s32[896]{0:T(1024)S(1)}, s32[896]{0:T(1024)S(1)}, u32[]{:S(2)}, u32[]{:S(2)}) collective-permute-start(s32[896]{0:T(1024)S(1)} %pad_add_fusion.3), channel_id=1, source_target_pairs={{0,12},{2,14},{4,0},{6,2},{8,4},{10,6},{12,8},{14,10},{1,13},{3,15... | collective-permute-start | bytes 10760 | tf_op jit(solution)/shard_map/ppermute | solution.py:207
  9.0 5.8 %collective-permute-start = (bf16[4096]{0:T(1024)(128)(2,1)}, bf16[4096]{0:T(1024)(128)(2,1)S(1)}, u32[]{:S(2)}, u32[]{:S(2)}) collective-permute-start(bf16[4096]{0:T(1024)(128)(2,1)} %param.11), channel_id=1, source_target_pairs={{0,1},{1,0},{2,3},{3,2},{4,5},{5,4},{6,7},{7,6},{8,9},{9,8},{10,11... | collective-permute-start | bytes 24584 | tf_op jit(solution)/shard_map/ppermute | solution.py:202
  10.5 17.7 %collective-permute-start.7 = (bf16[4096,128]{1,0:T(8,128)(2,1)}, bf16[4096,128]{1,0:T(8,128)(2,1)S(1)}, u32[]{:S(2)}, u32[]{:S(2)}) collective-permute-start(bf16[4096,128]{1,0:T(8,128)(2,1)} %wk_ref.1), channel_id=1, source_target_pairs={{0,1},{1,0},{2,3},{3,2},{4,5},{5,4},{6,7},{7,6},{8,9},{9,8},{10,11... | collective-permute-start | bytes 3145736 | tf_op jit(solution)/shard_map/ppermute | solution.py:202
  11.1 17.1 %collective-permute-start.8 = (bf16[4096,128]{1,0:T(8,128)(2,1)}, bf16[4096,128]{1,0:T(8,128)(2,1)}, u32[]{:S(2)}, u32[]{:S(2)}) collective-permute-start(bf16[4096,128]{1,0:T(8,128)(2,1)} %wv_ref.1), channel_id=1, source_target_pairs={{0,1},{1,0},{2,3},{3,2},{4,5},{5,4},{6,7},{7,6},{8,9},{9,8},{10,11... | collective-permute-start | bytes 3145736 | tf_op jit(solution)/shard_map/ppermute | solution.py:202
  11.2 3.8 %collective-permute-start.5 = (s32[4,896]{1,0:T(4,128)S(1)}, s32[4,896]{1,0:T(4,128)S(1)}, u32[]{:S(2)}, u32[]{:S(2)}) collective-permute-start(s32[4,896]{1,0:T(4,128)S(1)} %pad_add_fusion.2), channel_id=1, source_target_pairs={{0,2},{2,0},{4,6},{6,4},{8,10},{10,8},{12,14},{14,12},{1,3},{3,1},... | collective-permute-start | bytes 43016 | tf_op jit(solution)/shard_map/ppermute | solution.py:212
  15.7 10.2 %collective-permute-start.6 = (s32[8,896]{1,0:T(8,128)}, s32[8,896]{1,0:T(8,128)S(1)}, u32[]{:S(2)}, u32[]{:S(2)}) collective-permute-start(s32[8,896]{1,0:T(8,128)} %concatenate.52), channel_id=1, source_target_pairs={{0,1},{1,0},{2,3},{3,2},{4,5},{5,4},{6,7},{7,6},{8,9},{9,8},{10,11... | collective-permute-start | bytes 86024 | tf_op jit(solution)/shard_map/ppermute | solution.py:202
  32.5 38.6 %copy-start.7 = (bf16[256,256]{1,0:T(8,128)(2,1)}, bf16[256,256]{1,0:T(8,128)(2,1)S(1)}, u32[]{:S(2)}) copy-start(bf16[256,256]{1,0:T(8,128)(2,1)S(1)} %keys_values.1.rest_0_) | copy-start | bytes 393220
  32.5 8.2 %collective-permute-start.9 = (bf16[256,256]{1,0:T(8,128)(2,1)S(1)}, bf16[256,256]{1,0:T(8,128)(2,1)S(1)}, u32[]{:S(2)}, u32[]{:S(2)}) collective-permute-start(bf16[256,256]{1,0:T(8,128)(2,1)S(1)} %keys_values.1.rest_0_), channel_id=1, source_target_pairs={{0,4},{2,6},{4,8},{6,10},{8,12},{10,14},{12,0},{14,2},{1,5},{3,7},... | collective-permute-start | bytes 393224 | tf_op jit(solution)/shard_map/ppermute | solution.py:207
  33.2 12.8 %collective-permute-start.10 = (bf16[256,256]{1,0:T(8,128)(2,1)S(1)}, bf16[256,256]{1,0:T(8,128)(2,1)S(1)}, u32[]{:S(2)}, u32[]{:S(2)}) collective-permute-start(bf16[256,256]{1,0:T(8,128)(2,1)S(1)} %keys_values.1.rest_0_), channel_id=1, source_target_pairs={{0,8},{2,10},{4,12},{6,14},{8,0},{10,2},{12,4},{14,6},{1,9},{3,11}... | collective-permute-start | bytes 393224 | tf_op jit(solution)/shard_map/ppermute | solution.py:207
  37.8 11.2 %collective-permute-start.11 = (bf16[256,256]{1,0:T(8,128)(2,1)S(1)}, bf16[256,256]{1,0:T(8,128)(2,1)S(1)}, u32[]{:S(2)}, u32[]{:S(2)}) collective-permute-start(bf16[256,256]{1,0:T(8,128)(2,1)S(1)} %keys_values.1.rest_0_), channel_id=1, source_target_pairs={{0,12},{2,14},{4,0},{6,2},{8,4},{10,6},{12,8},{14,10},{1,13},{3,15... | collective-permute-start | bytes 393224 | tf_op jit(solution)/shard_map/ppermute | solution.py:207
  38.2 10.8 %collective-permute-start.12 = (bf16[256,256]{1,0:T(8,128)(2,1)S(1)}, bf16[256,256]{1,0:T(8,128)(2,1)S(1)}, u32[]{:S(2)}, u32[]{:S(2)}) collective-permute-start(bf16[256,256]{1,0:T(8,128)(2,1)S(1)} %keys_values.1.rest_0_), channel_id=1, source_target_pairs={{0,2},{2,0},{4,6},{6,4},{8,10},{10,8},{12,14},{14,12},{1,3},{3,1},... | collective-permute-start | bytes 393224 | tf_op jit(solution)/shard_map/ppermute | solution.py:212
  40.8 30.3 %copy-start.15 = (bf16[256,256]{1,0:T(8,128)(2,1)}, bf16[256,256]{1,0:T(8,128)(2,1)S(1)}, u32[]{:S(2)}) copy-start(bf16[256,256]{1,0:T(8,128)(2,1)S(1)} %collective-permute-done.9.rest_1_) | copy-start | bytes 393220
  40.8 8.8 %collective-permute-start.16 = (bf16[256,256]{1,0:T(8,128)(2,1)S(1)}, bf16[256,256]{1,0:T(8,128)(2,1)S(1)}, u32[]{:S(2)}, u32[]{:S(2)}) collective-permute-start(bf16[256,256]{1,0:T(8,128)(2,1)S(1)} %keys_values.1.rest_0_), channel_id=1, source_target_pairs={{0,1},{1,0},{2,3},{3,2},{4,5},{5,4},{6,7},{7,6},{8,9},{9,8},{10,11... | collective-permute-start | bytes 393224 | tf_op jit(solution)/shard_map/ppermute | solution.py:202
  46.0 25.1 %copy-start.16 = (bf16[256,256]{1,0:T(8,128)(2,1)}, bf16[256,256]{1,0:T(8,128)(2,1)S(1)}, u32[]{:S(2)}) copy-start(bf16[256,256]{1,0:T(8,128)(2,1)S(1)} %collective-permute-done.10.rest_2_) | copy-start | bytes 393220
  46.0 5.1 %collective-permute-start.13 = (bf16[256,256]{1,0:T(8,128)(2,1)S(1)}, bf16[256,256]{1,0:T(8,128)(2,1)S(1)}, u32[]{:S(2)}, u32[]{:S(2)}) collective-permute-start(bf16[256,256]{1,0:T(8,128)(2,1)S(1)} %collective-permute-done.9.rest_1_), channel_id=1, source_target_pairs={{0,2},{2,0},{4,6},{6,4},{8,10},{10,8},{12,14},{14,12},{1,3},{3,1},... | collective-permute-start | bytes 393224 | tf_op jit(solution)/shard_map/ppermute | solution.py:212
  49.0 22.1 %copy-start.17 = (bf16[256,256]{1,0:T(8,128)(2,1)}, bf16[256,256]{1,0:T(8,128)(2,1)S(1)}, u32[]{:S(2)}) copy-start(bf16[256,256]{1,0:T(8,128)(2,1)S(1)} %collective-permute-done.11.rest_3_) | copy-start | bytes 393220
  49.0 8.9 %collective-permute-start.17 = (bf16[256,256]{1,0:T(8,128)(2,1)S(1)}, bf16[256,256]{1,0:T(8,128)(2,1)S(1)}, u32[]{:S(2)}, u32[]{:S(2)}) collective-permute-start(bf16[256,256]{1,0:T(8,128)(2,1)S(1)} %collective-permute-done.9.rest_1_), channel_id=1, source_target_pairs={{0,1},{1,0},{2,3},{3,2},{4,5},{5,4},{6,7},{7,6},{8,9},{9,8},{10,11... | collective-permute-start | bytes 393224 | tf_op jit(solution)/shard_map/ppermute | solution.py:202
  49.0 22.1 %copy-start.18 = (bf16[256,256]{1,0:T(8,128)(2,1)}, bf16[256,256]{1,0:T(8,128)(2,1)S(1)}, u32[]{:S(2)}) copy-start(bf16[256,256]{1,0:T(8,128)(2,1)S(1)} %collective-permute-done.12.rest_4_) | copy-start | bytes 393220
  49.0 6.5 %collective-permute-start.14 = (bf16[256,256]{1,0:T(8,128)(2,1)S(1)}, bf16[256,256]{1,0:T(8,128)(2,1)}, u32[]{:S(2)}, u32[]{:S(2)}) collective-permute-start(bf16[256,256]{1,0:T(8,128)(2,1)S(1)} %collective-permute-done.10.rest_2_), channel_id=1, source_target_pairs={{0,2},{2,0},{4,6},{6,4},{8,10},{10,8},{12,14},{14,12},{1,3},{3,1},... | collective-permute-start | bytes 393224 | tf_op jit(solution)/shard_map/ppermute | solution.py:212
  49.6 8.8 %collective-permute-start.18 = (bf16[256,256]{1,0:T(8,128)(2,1)S(1)}, bf16[256,256]{1,0:T(8,128)(2,1)S(1)}, u32[]{:S(2)}, u32[]{:S(2)}) collective-permute-start(bf16[256,256]{1,0:T(8,128)(2,1)S(1)} %collective-permute-done.10.rest_2_), channel_id=1, source_target_pairs={{0,1},{1,0},{2,3},{3,2},{4,5},{5,4},{6,7},{7,6},{8,9},{9,8},{10,11... | collective-permute-start | bytes 393224 | tf_op jit(solution)/shard_map/ppermute | solution.py:202
  51.1 6.7 %collective-permute-start.15 = (bf16[256,256]{1,0:T(8,128)(2,1)S(1)}, bf16[256,256]{1,0:T(8,128)(2,1)}, u32[]{:S(2)}, u32[]{:S(2)}) collective-permute-start(bf16[256,256]{1,0:T(8,128)(2,1)S(1)} %collective-permute-done.11.rest_3_), channel_id=1, source_target_pairs={{0,2},{2,0},{4,6},{6,4},{8,10},{10,8},{12,14},{14,12},{1,3},{3,1},... | collective-permute-start | bytes 393224 | tf_op jit(solution)/shard_map/ppermute | solution.py:212
  55.5 16.3 %collective-permute-start.19 = (bf16[256,256]{1,0:T(8,128)(2,1)S(1)}, bf16[256,256]{1,0:T(8,128)(2,1)}, u32[]{:S(2)}, u32[]{:S(2)}) collective-permute-start(bf16[256,256]{1,0:T(8,128)(2,1)S(1)} %collective-permute-done.11.rest_3_), channel_id=1, source_target_pairs={{0,1},{1,0},{2,3},{3,2},{4,5},{5,4},{6,7},{7,6},{8,9},{9,8},{10,11... | collective-permute-start | bytes 393224 | tf_op jit(solution)/shard_map/ppermute | solution.py:202
  57.8 14.0 %collective-permute-start.20 = (bf16[256,256]{1,0:T(8,128)(2,1)S(1)}, bf16[256,256]{1,0:T(8,128)(2,1)}, u32[]{:S(2)}, u32[]{:S(2)}) collective-permute-start(bf16[256,256]{1,0:T(8,128)(2,1)S(1)} %collective-permute-done.12.rest_4_), channel_id=1, source_target_pairs={{0,1},{1,0},{2,3},{3,2},{4,5},{5,4},{6,7},{7,6},{8,9},{9,8},{10,11... | collective-permute-start | bytes 393224 | tf_op jit(solution)/shard_map/ppermute | solution.py:202
  57.9 14.0 %collective-permute-start.21 = (bf16[256,256]{1,0:T(8,128)(2,1)S(1)}, bf16[256,256]{1,0:T(8,128)(2,1)}, u32[]{:S(2)}, u32[]{:S(2)}) collective-permute-start(bf16[256,256]{1,0:T(8,128)(2,1)S(1)} %collective-permute-done.13.rest_5_), channel_id=1, source_target_pairs={{0,1},{1,0},{2,3},{3,2},{4,5},{5,4},{6,7},{7,6},{8,9},{9,8},{10,11... | collective-permute-start | bytes 393224 | tf_op jit(solution)/shard_map/ppermute | solution.py:202
  58.4 13.5 %collective-permute-start.22 = (bf16[256,256]{1,0:T(8,128)(2,1)}, bf16[256,256]{1,0:T(8,128)(2,1)}, u32[]{:S(2)}, u32[]{:S(2)}) collective-permute-start(bf16[256,256]{1,0:T(8,128)(2,1)} %collective-permute-done.14.rest_6_), channel_id=1, source_target_pairs={{0,1},{1,0},{2,3},{3,2},{4,5},{5,4},{6,7},{7,6},{8,9},{9,8},{10,11... | collective-permute-start | bytes 393224 | tf_op jit(solution)/shard_map/ppermute | solution.py:202
  58.5 13.4 %collective-permute-start.23 = (bf16[256,256]{1,0:T(8,128)(2,1)}, bf16[256,256]{1,0:T(8,128)(2,1)}, u32[]{:S(2)}, u32[]{:S(2)}) collective-permute-start(bf16[256,256]{1,0:T(8,128)(2,1)} %collective-permute-done.15.rest_7_), channel_id=1, source_target_pairs={{0,1},{1,0},{2,3},{3,2},{4,5},{5,4},{6,7},{7,6},{8,9},{9,8},{10,11... | collective-permute-start | bytes 393224 | tf_op jit(solution)/shard_map/ppermute | solution.py:202
  (17 other events, 77.7 us)
